TPU v7x, 32 devices: a whole 2x2x4 slice. The times are simulated.
32 devices in a mesh: parts: 2 (over x), rows: 16 (over z, y, core).
Axes of the slice: x: 2, y: 2, z: 4, core: 2. Of those that a mesh axis runs over, the one named last changes fastest.
Arguments:
- gain_tiles: float32 [4, 8192, 3, 128], P(None, ('parts', 'rows')), parts along dimension 1, may hold values from -0.21875 to 0.21875
- tile_pattern: int32 [8, 32, 3], P('parts'), parts along dimension 0, may hold values from 0 to 31, as said below
- offset_terms: float32 [4, 8192], P(None, ('parts', 'rows')), parts along dimension 1, may hold values from -6 to 6
- last_mean: float32 [8192], P(('parts', 'rows')), parts along dimension 0, may hold values from -6 to 6
- last_covariance: float32 [8192, 4096], P(('parts', 'rows')), parts along dimension 0, as said below
- noise_covariance: float32 [4, 8192, 4096], P(None, ('parts', 'rows')), parts along dimension 1, as said below
Outputs:
- smoothed_covariance: float32 [4, 8192, 4096], P(None, ('parts', 'rows')), parts along dimension 1
- smoothed_mean: float32 [4, 8192], P(None, ('parts', 'rows')), parts along dimension 1
There are 2 independent parts, one for each index of `parts`. A program takes and returns all parts, laid end to end along the dimension named above; each array names one. Nothing has to cross between parts.
Inputs may be any that keep to these rules, and one draw needn't show every extreme that they name: `tile_pattern`: each tile row names 3 different tile columns; the first is the tile row's own number. `last_covariance`: symmetric. `noise_covariance`: each block's matrix is symmetric.
All inputs are finite; a program needn't handle non-finite values.
Results may differ from a plain program's by a relative error of at most 0.0001.
Values sent between devices are 32-bit elements; how exact they have to be, the bound alone decides.
A program may use at most 192 MiB of HBM per device.

v0:
```python
import jax
import jax.numpy as jnp
from jax import lax
from jax.sharding import PartitionSpec as P

WIDTH = 4096
TILE = 128
PER_ROW = 3
BLOCKS = 4
TILE_ROWS = 32


def right_product(dense_rows, gain_values, pattern_block):
    row_count = dense_rows.shape[0]
    tiled = dense_rows.reshape(row_count, TILE_ROWS, TILE)
    picked = tiled[:, pattern_block, :]
    shaped = gain_values.reshape(TILE_ROWS, TILE, PER_ROW, TILE)
    result = jnp.einsum("rtkj,tckj->rtc", picked, shaped, precision=lax.Precision.HIGHEST)
    return result.reshape(row_count, WIDTH)


def left_product(columns, gain_values, pattern_block):
    column_count = columns.shape[1]
    tiled = columns.reshape(TILE_ROWS, TILE, column_count)
    picked = tiled[pattern_block]
    shaped = gain_values.reshape(TILE_ROWS, TILE, PER_ROW, TILE)
    result = jnp.einsum("tkjc,tqkj->ctq", picked, shaped, precision=lax.Precision.HIGHEST)
    return result.reshape(column_count, WIDTH)


def shards(gain_tiles, tile_pattern, offset_terms, last_mean, last_covariance, noise_covariance):
    local_rows = last_mean.shape[0]
    first_row = lax.axis_index("rows") * local_rows
    row_numbers = first_row + jnp.arange(local_rows, dtype=jnp.int32)
    tile_match = (
        row_numbers[:, None] // TILE == jnp.arange(TILE_ROWS, dtype=jnp.int32)[None, :]
    ).astype(jnp.int32)
    current_mean = last_mean
    covariance = last_covariance
    cov_list = []
    mean_list = []
    for block_index in reversed(range(BLOCKS)):
        pattern_block = tile_pattern[block_index]
        gain_values = lax.all_gather(gain_tiles[block_index], "rows", axis=0, tiled=True)
        partial_image = right_product(covariance, gain_values, pattern_block)
        received = lax.all_to_all(partial_image, "rows", split_axis=1, concat_axis=0, tiled=True)
        covariance = (
            left_product(received, gain_values, pattern_block) + noise_covariance[block_index]
        )
        cov_list.append(covariance)
        gathered_mean = lax.all_gather(current_mean, "rows", axis=0, tiled=True)
        mean_tiles = gathered_mean.reshape(TILE_ROWS, TILE)
        own_pattern = jnp.sum(tile_match[:, :, None] * pattern_block[None, :, :], axis=1)
        picked = mean_tiles[own_pattern]
        current_mean = (
            jnp.sum(picked * gain_tiles[block_index], axis=(1, 2)) + offset_terms[block_index]
        )
        mean_list.append(current_mean)
    cov_list = cov_list[::-1]
    mean_list = mean_list[::-1]
    return (jnp.stack(cov_list, 0), jnp.stack(mean_list, 0))


def solution(mesh):
    in_specs = (
        P(None, ("parts", "rows"), None, None),
        P("parts", None, None),
        P(None, ("parts", "rows")),
        P(("parts", "rows")),
        P(("parts", "rows"), None),
        P(None, ("parts", "rows"), None),
    )
    out_specs = (P(None, ("parts", "rows"), None), P(None, ("parts", "rows")))
    return jax.shard_map(shards, mesh=mesh, in_specs=in_specs, out_specs=out_specs, check_vma=False)
```

profile of v0, /device:TPU:0, one launch (start us, length us, event | category | flops | bytes accessed | tf_op | source)
XLA Modules:
  0.0 974.5 jit_solution(8600243610957248146)
XLA Ops:
  22.0 11.3 %gather_fusion = f32[96,256,128]{2,1,0:T(8,128)} fusion(f32[256,32,128]{2,0,1:T(8,128)} %copy.139, s32[1024]{0:T(1024)S(1)} %pad_clamp_fusion.7), kind=kCustom, calls=%fused_computation | custom fusion | bytes 25166208 | tf_op jit(solution)/shard_map/gather | solution.py:16
  33.3 41.6 %all-gather.13.cloned.1.call-done = f32[1,4096,3,128]{3,1,2,0:T(8,128)} async-done(((f32[1,256,3,128]{3,1,2,0:T(8,128)}), f32[1,4096,3,128]{3,1,2,0:T(8,128)}) %all-gather.13.cloned.1.call-update) | async-done | bytes 6291472 | tf_op jit(solution)/shard_map/all_gather | solution.py:44
  74.9 21.4 %fusion.17 = f32[32,256,128,1]{1,2,3,0:T(8,128)} fusion(f32[256,32,3,128]{3,0,2,1:T(8,128)} %bitcast.173, f32[32,128,3,128]{3,1,0,2:T(8,128)} %bitcast.184), kind=kOutput, calls=%fused_computation.30 | convolution fusion | flops 4831838208 | bytes 23068672 | tf_op jit(solution)/shard_map/rtkj,tckj->rtc/dot_general | solution.py:18
  122.6 97.4 %all-to-all-done = f32[256,16,256]{2,0,1:T(8,128)} async-done(((f32[256,16,256]{2,0,1:T(8,128)}), f32[256,16,256]{2,0,1:T(8,128)}, u32[]{:S(2)}, u32[]{:S(2)}) %all-to-all-start) | async-done | bytes 4194336 | tf_op jit(solution)/shard_map/all_to_all | solution.py:46
  231.1 15.4 %bitcast_add_fusion = (f32[256,32,128]{0,2,1:T(8,128)}, f32[32,256,128,1]{1,2,3,0:T(8,128)}) fusion(f32[256,32,128]{0,2,1:T(8,128)} %bitcast.190, f32[32,3,128,256]{3,2,1,0:T(8,128)} %bitcast.174, f32[32,128,3,128]{3,1,0,2:T(8,128)} %bitcast.185), kind=kOutput, calls=%fused_computation.32 | convolution fusion | flops 4832886784 | bytes 31457280 | tf_op jit(solution)/shard_map/tkjc,tqkj->ctq/dot_general | solution.py:27
  257.7 12.7 %copy.145 = f32[32,3,256,128]{3,2,1,0:T(8,128)} copy(f32[32,3,256,128]{2,3,1,0:T(8,128)} %bitcast.170) | data formatting | bytes 25165824 | tf_op jit(solution)/shard_map/gather | solution.py:16
  270.5 21.4 %fusion.4 = f32[32,256,128,1]{1,2,3,0:T(8,128)} fusion(f32[32,3,256,128]{3,2,1,0:T(8,128)} %copy.145, f32[32,128,3,128]{3,1,0,2:T(8,128)} %bitcast.182), kind=kOutput, calls=%fused_computation.17 | convolution fusion | flops 4831838208 | bytes 23068672 | tf_op jit(solution)/shard_map/rtkj,tckj->rtc/dot_general | solution.py:18
  297.3 40.2 %all-to-all-start.1 = ((f32[256,16,256]{2,0,1:T(8,128)}), f32[256,16,256]{2,0,1:T(8,128)}, u32[]{:S(2)}, u32[]{:S(2)}) async-start(f32[256,16,256]{2,0,1:T(8,128)} %copy.147), calls=%async_computation.1 | async-start | bytes 8388608 | tf_op jit(solution)/shard_map/all_to_all | solution.py:46
  344.1 108.9 %all-to-all-done.1 = f32[256,16,256]{2,0,1:T(8,128)} async-done(((f32[256,16,256]{2,0,1:T(8,128)}), f32[256,16,256]{2,0,1:T(8,128)}, u32[]{:S(2)}, u32[]{:S(2)}) %all-to-all-start.1) | async-done | bytes 4194336 | tf_op jit(solution)/shard_map/all_to_all | solution.py:46
  464.2 15.3 %bitcast_add_fusion.1 = (f32[256,32,128]{0,2,1:T(8,128)}, f32[32,256,128,1]{1,2,3,0:T(8,128)}) fusion(f32[256,32,128]{0,2,1:T(8,128)} %bitcast.191, f32[32,3,128,256]{3,2,1,0:T(8,128)} %bitcast.175, f32[32,128,3,128]{3,1,0,2:T(8,128)} %bitcast.183), kind=kOutput, calls=%fused_computation.33 | convolution fusion | flops 4832886784 | bytes 31457280 | tf_op jit(solution)/shard_map/tkjc,tqkj->ctq/dot_general | solution.py:27
  490.5 13.0 %copy.151 = f32[32,3,256,128]{3,2,1,0:T(8,128)} copy(f32[32,3,256,128]{2,3,1,0:T(8,128)} %bitcast.171) | data formatting | bytes 25165824 | tf_op jit(solution)/shard_map/gather | solution.py:16
  503.5 21.4 %fusion.2 = f32[32,256,128,1]{1,2,3,0:T(8,128)} fusion(f32[32,3,256,128]{3,2,1,0:T(8,128)} %copy.151, f32[32,128,3,128]{3,1,0,2:T(8,128)} %bitcast.180), kind=kOutput, calls=%fused_computation.15 | convolution fusion | flops 4831838208 | bytes 23068672 | tf_op jit(solution)/shard_map/rtkj,tckj->rtc/dot_general | solution.py:18
  530.3 19.9 %all-to-all-start.2 = ((f32[256,16,256]{2,0,1:T(8,128)}), f32[256,16,256]{2,0,1:T(8,128)}, u32[]{:S(2)}, u32[]{:S(2)}) async-start(f32[256,16,256]{2,0,1:T(8,128)} %copy.153), calls=%async_computation.2 | async-start | bytes 8388608 | tf_op jit(solution)/shard_map/all_to_all | solution.py:46
  556.1 71.8 %all-to-all-done.2 = f32[256,16,256]{2,0,1:T(8,128)} async-done(((f32[256,16,256]{2,0,1:T(8,128)}), f32[256,16,256]{2,0,1:T(8,128)}, u32[]{:S(2)}, u32[]{:S(2)}) %all-to-all-start.2) | async-done | bytes 4194336 | tf_op jit(solution)/shard_map/all_to_all | solution.py:46
  639.0 15.2 %bitcast_add_fusion.2 = (f32[256,32,128]{0,2,1:T(8,128)}, f32[32,256,128,1]{1,2,3,0:T(8,128)}) fusion(f32[256,32,128]{0,2,1:T(8,128)} %bitcast.189, f32[32,3,128,256]{3,2,1,0:T(8,128)} %bitcast.176, f32[32,128,3,128]{3,1,0,2:T(8,128)} %bitcast.181), kind=kOutput, calls=%fused_computation.34 | convolution fusion | flops 4832886784 | bytes 31457280 | tf_op jit(solution)/shard_map/tkjc,tqkj->ctq/dot_general | solution.py:27
  665.4 12.8 %copy.157 = f32[32,3,256,128]{3,2,1,0:T(8,128)} copy(f32[32,3,256,128]{2,3,1,0:T(8,128)} %bitcast.172) | data formatting | bytes 25165824 | tf_op jit(solution)/shard_map/gather | solution.py:16
  678.2 21.4 %fusion = f32[32,256,128,1]{1,2,3,0:T(8,128)} fusion(f32[32,3,256,128]{3,2,1,0:T(8,128)} %copy.157, f32[32,128,3,128]{3,1,0,2:T(8,128)} %bitcast.178), kind=kOutput, calls=%fused_computation.13 | convolution fusion | flops 4831838208 | bytes 23068672 | tf_op jit(solution)/shard_map/rtkj,tckj->rtc/dot_general | solution.py:18
  704.9 20.1 %all-to-all-start.3 = ((f32[256,16,256]{2,0,1:T(8,128)}), f32[256,16,256]{2,0,1:T(8,128)}, u32[]{:S(2)}, u32[]{:S(2)}) async-start(f32[256,16,256]{2,0,1:T(8,128)} %copy.159), calls=%async_computation.3 | async-start | bytes 8388608 | tf_op jit(solution)/shard_map/all_to_all | solution.py:46
  725.7 83.4 %all-gather.4 = f32[16,1,256]{2,1,0:T(1,128)S(1)} all-gather(f32[1,1,256]{2,1,0:T(1,128)S(1)} %bitcast.208), channel_id=1, replica_groups=mesh['parts'=2,'rows'=16] {'rows'}, dimensions={0}, use_global_device_ids=true | all-gather | bytes 17408 | tf_op jit(solution)/shard_map/all_gather | solution.py:51
  811.3 38.4 %all-gather.5 = f32[16,1,256]{2,1,0:T(1,128)S(1)} all-gather(f32[1,1,256]{2,1,0:T(1,128)S(1)} %bitcast.201), channel_id=1, replica_groups=mesh['parts'=2,'rows'=16] {'rows'}, dimensions={0}, use_global_device_ids=true | all-gather | bytes 17408 | tf_op jit(solution)/shard_map/all_gather | solution.py:51
  852.0 17.4 %all-gather.6 = f32[16,1,256]{2,1,0:T(1,128)S(1)} all-gather(f32[1,1,256]{2,1,0:T(1,128)S(1)} %bitcast.202), channel_id=1, replica_groups=mesh['parts'=2,'rows'=16] {'rows'}, dimensions={0}, use_global_device_ids=true | all-gather | bytes 17408 | tf_op jit(solution)/shard_map/all_gather | solution.py:51
  871.7 18.8 %all-gather.7 = f32[16,1,256]{2,1,0:T(1,128)S(1)} all-gather(f32[1,1,256]{2,1,0:T(1,128)S(1)} %bitcast.203), channel_id=1, replica_groups=mesh['parts'=2,'rows'=16] {'rows'}, dimensions={0}, use_global_device_ids=true | all-gather | bytes 17408 | tf_op jit(solution)/shard_map/all_gather | solution.py:51
  921.0 14.0 %fusion.6 = f32[32,256,128,1]{1,2,3,0:T(8,128)} fusion(f32[32,3,128,256]{3,2,1,0:T(8,128)} %bitcast.177, f32[32,128,3,128]{3,1,0,2:T(8,128)} %bitcast.179), kind=kOutput, calls=%fused_computation.19 | convolution fusion | flops 4831838208 | bytes 23068672 | tf_op jit(solution)/shard_map/tkjc,tqkj->ctq/dot_general | solution.py:27
  940.6 16.2 %slice_add_fusion = (f32[1,256,4096]{2,1,0:T(8,128)S(1)}, f32[1,256,4096]{2,1,0:T(8,128)}, f32[1,256,4096]{2,1,0:T(8,128)}, f32[1,256,4096]{2,1,0:T(8,128)}) fusion(f32[1,256,4096]{2,1,0:T(8,128)} %copy.161, f32[4,256,4096]{2,1,0:T(8,128)} %param.11, f32[1,256,4096]{2,1,0:T(8,128)} %copy.164, f32[1,256,4096]{2,1,0:T(8,128)} %copy.163, f32[1,256,4096]{2,1,0:T(8,128)} %copy.162), kind=kLoop, calls=%fused_computation.35 | loop fusion | flops 4194304 | bytes 50331648 | tf_op jit(solution)/shard_map/add | solution.py:48
  (99 shorter events, 190.3 us)
Async XLA Ops:
  7.2 67.7 %all-gather.13.cloned.1.call-start = ((), (), s32[]{:S(2)}) async-start(), calls=%async_computation.4 | async-start | bytes 6684672 | tf_op jit(solution)/shard_map/all_gather | solution.py:44
  9.8 260.7 %all-gather.15.cloned.1.call-start = ((), (), s32[]{:S(2)}) async-start(), calls=%async_computation.5 | async-start | bytes 6684672 | tf_op jit(solution)/shard_map/all_gather | solution.py:44
  16.1 5.6 copy-start.1
  101.7 118.3 %all-to-all-start = ((f32[256,16,256]{2,0,1:T(8,128)}), f32[256,16,256]{2,0,1:T(8,128)}, u32[]{:S(2)}, u32[]{:S(2)}) async-start(f32[256,16,256]{2,0,1:T(8,128)} %copy.141), calls=%async_computation | async-start | bytes 8388608 | tf_op jit(solution)/shard_map/all_to_all | solution.py:46
  106.2 397.3 %all-gather.17.cloned.1.call-start = ((), (), s32[]{:S(2)}) async-start(), calls=%async_computation.6 | async-start | bytes 6684672 | tf_op jit(solution)/shard_map/all_gather | solution.py:44
  297.3 155.8 %all-to-all-start.1 = ((f32[256,16,256]{2,0,1:T(8,128)}), f32[256,16,256]{2,0,1:T(8,128)}, u32[]{:S(2)}, u32[]{:S(2)}) async-start(f32[256,16,256]{2,0,1:T(8,128)} %copy.147), calls=%async_computation.1 | async-start | bytes 8388608 | tf_op jit(solution)/shard_map/all_to_all | solution.py:46
  337.5 340.6 %all-gather.19.cloned.1.call-start = ((), (), s32[]{:S(2)}) async-start(), calls=%async_computation.7 | async-start | bytes 6684672 | tf_op jit(solution)/shard_map/all_gather | solution.py:44
  530.3 97.6 %all-to-all-start.2 = ((f32[256,16,256]{2,0,1:T(8,128)}), f32[256,16,256]{2,0,1:T(8,128)}, u32[]{:S(2)}, u32[]{:S(2)}) async-start(f32[256,16,256]{2,0,1:T(8,128)} %copy.153), calls=%async_computation.2 | async-start | bytes 8388608 | tf_op jit(solution)/shard_map/all_to_all | solution.py:46
  704.9 20.1 %copy-start.2 = (s32[4,32,3]{1,0,2:T(4,128)S(1)}, s32[4,32,3]{1,0,2:T(4,128)}, u32[]{:S(2)}) copy-start(s32[4,32,3]{1,0,2:T(4,128)} %param.7) | copy-start | bytes 4612
  704.9 20.7 %copy-start.4 = (f32[256]{0:T(256)S(1)}, f32[256]{0:T(256)}, u32[]{:S(2)}) copy-start(f32[256]{0:T(256)} %param.9) | copy-start | bytes 3076
  704.9 106.2 %copy-start = (f32[4,256,3,128]{3,1,2,0:T(8,128)S(1)}, f32[4,256,3,128]{3,1,2,0:T(8,128)}, u32[]{:S(2)}) copy-start(f32[4,256,3,128]{3,1,2,0:T(8,128)} %param.6) | copy-start | bytes 4718596
  704.9 106.3 %copy-start.3 = (f32[4,256]{1,0:T(4,128)S(1)}, f32[4,256]{1,0:T(4,128)}, u32[]{:S(2)}) copy-start(f32[4,256]{1,0:T(4,128)} %param.8) | copy-start | bytes 12292
  704.9 205.0 %all-to-all-start.3 = ((f32[256,16,256]{2,0,1:T(8,128)}), f32[256,16,256]{2,0,1:T(8,128)}, u32[]{:S(2)}, u32[]{:S(2)}) async-start(f32[256,16,256]{2,0,1:T(8,128)} %copy.159), calls=%async_computation.3 | async-start | bytes 8388608 | tf_op jit(solution)/shard_map/all_to_all | solution.py:46
Sparse Core Ops, SparseCore 0:
  10.2 64.6 all-gather.12
  77.0 95.2 all-gather.14
  174.5 88.5 all-gather.16
  340.2 108.7 all-gather.18
where the time goes:
time: 979 us; the launch traced here: 974 us
  waiting for transfers between devices  321 us (33%)
  local copies, waits for them, and re-layouts  221 us (23%)
  blocking collectives  158 us (16%)
  matrix products  146 us (15%)
  starting transfers between devices  85.4 us (9%)
  other arithmetic  28.3 us (3%)
  between operations  14.6 us (1%)
    all_to_all x4, waiting for transfers between devices, shards(): lax.all_to_all(partial_image, 'rows', split_axis=1, concat_axis=0, tiled=...  278 us
    all_gather x4, blocking collectives, shards(): gathered_mean = lax.all_gather(current_mean, 'rows', axis=0, tiled=True)  158 us
    dot_general x4, matrix products, right_product(): jnp.einsum('rtkj,tckj->rtc', picked, shaped, precision=lax.Precision.HIGH...  85.7 us
    all_to_all x4, starting transfers between devices, shards(): lax.all_to_all(partial_image, 'rows', split_axis=1, concat_axis=0, tiled=...  84.8 us
    gather x7, local copies, waits for them, and re-layouts, right_product(): picked = tiled[:, pattern_block, :]  83.1 us
    dot_general x4, matrix products, left_product(): jnp.einsum('tkjc,tqkj->ctq', picked, shaped, precision=lax.Precision.HIGH...  59.8 us
    gather x4, local copies, waits for them, and re-layouts, left_product(): picked = tiled[pattern_block]  44.4 us
    all_gather x4, waiting for transfers between devices, shards(): lax.all_gather(gain_tiles[block_index], 'rows', axis=0, tiled=True)  41.7 us
  transfers between devices with their start and end apart: 8, of which 4 were waited for; matrix products, arithmetic and copies ran while one was open for 32% of the time, Pallas kernels for 0%

commit v1 on v0

--- a/solution.py
+++ b/solution.py
@@ -8,6 +8,22 @@
 PER_ROW = 3
 BLOCKS = 4
 TILE_ROWS = 32
+
+
+def gather_around(x, axis, dim):
+    ways, here, turn = (lax.axis_size(axis), lax.axis_index(axis), x.shape[dim])
+    shape = [n * ways if d == dim else n for d, n in enumerate(x.shape)]
+    full = lax.dynamic_update_slice_in_dim(jnp.zeros(shape, x.dtype), x, here * turn, axis=dim)
+    going_up = going_down = x
+    for far in range(1, ways // 2 + 1):
+        going_up = lax.ppermute(going_up, axis, [(d, (d + 1) % ways) for d in range(ways)])
+        full = lax.dynamic_update_slice_in_dim(full, going_up, (here - far) % ways * turn, axis=dim)
+        if 2 * far < ways:
+            going_down = lax.ppermute(going_down, axis, [(d, (d - 1) % ways) for d in range(ways)])
+            full = lax.dynamic_update_slice_in_dim(
+                full, going_down, (here + far) % ways * turn, axis=dim
+            )
+    return full
 
 
 def right_product(dense_rows, gain_values, pattern_block):
@@ -41,7 +57,7 @@
     mean_list = []
     for block_index in reversed(range(BLOCKS)):
         pattern_block = tile_pattern[block_index]
-        gain_values = lax.all_gather(gain_tiles[block_index], "rows", axis=0, tiled=True)
+        gain_values = gather_around(gain_tiles[block_index], "rows", 0)
         partial_image = right_product(covariance, gain_values, pattern_block)
         received = lax.all_to_all(partial_image, "rows", split_axis=1, concat_axis=0, tiled=True)
         covariance = (

time: 979 us -> 1130 us (1.15)
  the two profiles are of different devices: /device:TPU:0 before, /device:TPU:13 now
where the time goes in v1:
time: 1130 us; the launch traced here: 1120 us
  waiting for transfers between devices  414 us (37%)
  local copies, waits for them, and re-layouts  280 us (25%)
  starting transfers between devices  167 us (15%)
  matrix products  142 us (13%)
  blocking collectives  78.4 us (7%)
  other arithmetic  32.6 us (3%)
    ppermute x32, waiting for transfers between devices, gather_around(): lax.ppermute(going_up, axis, [(d, (d + 1) % ways) for d in range(ways)])  327 us
    dot_general x4, matrix products, right_product(): jnp.einsum('rtkj,tckj->rtc', picked, shaped, precision=lax.Precision.HIGH...  82.8 us
    gather x7, local copies, waits for them, and re-layouts, right_product(): picked = tiled[:, pattern_block, :]  82.7 us
    all_gather x4, blocking collectives, shards(): gathered_mean = lax.all_gather(current_mean, 'rows', axis=0, tiled=True)  78.4 us
    all_to_all x4, waiting for transfers between devices, shards(): lax.all_to_all(partial_image, 'rows', split_axis=1, concat_axis=0, tiled=...  74.8 us
    ppermute x32, starting transfers between devices, gather_around(): lax.ppermute(going_up, axis, [(d, (d + 1) % ways) for d in range(ways)])  73.5 us
    dot_general x4, matrix products, left_product(): jnp.einsum('tkjc,tqkj->ctq', picked, shaped, precision=lax.Precision.HIGH...  58.8 us
    ppermute x28, starting transfers between devices, gather_around(): lax.ppermute(going_down, axis, [(d, (d - 1) % ways) for d in range(ways)])  50.7 us
  transfers between devices with their start and end apart: 64, of which 31 were waited for; matrix products, arithmetic and copies ran while one was open for 13% of the time, Pallas kernels for 0%

profile of v1, /device:TPU:13, one launch (start us, length us, event | category | flops | bytes accessed | tf_op | source)
XLA Modules:
  0.0 1116.1 jit_solution(11514172593955072486)
XLA Ops:
  13.1 16.9 %all-gather = f32[16,1,256]{2,1,0:T(1,128)S(1)} all-gather(f32[1,1,256]{2,1,0:T(1,128)} %bitcast.206), channel_id=1, replica_groups=mesh['parts'=2,'rows'=16] {'rows'}, dimensions={0}, use_global_device_ids=true | all-gather | bytes 17408 | tf_op jit(solution)/shard_map/all_gather | solution.py:67
  39.2 23.8 %all-gather.1 = f32[16,1,256]{2,1,0:T(1,128)S(1)} all-gather(f32[1,1,256]{2,1,0:T(1,128)S(1)} %bitcast.199), channel_id=1, replica_groups=mesh['parts'=2,'rows'=16] {'rows'}, dimensions={0}, use_global_device_ids=true | all-gather | bytes 17408 | tf_op jit(solution)/shard_map/all_gather | solution.py:67
  71.9 18.6 %all-gather.2 = f32[16,1,256]{2,1,0:T(1,128)S(1)} all-gather(f32[1,1,256]{2,1,0:T(1,128)S(1)} %bitcast.200), channel_id=1, replica_groups=mesh['parts'=2,'rows'=16] {'rows'}, dimensions={0}, use_global_device_ids=true | all-gather | bytes 17408 | tf_op jit(solution)/shard_map/all_gather | solution.py:67
  96.9 19.0 %all-gather.3 = f32[16,1,256]{2,1,0:T(1,128)S(1)} all-gather(f32[1,1,256]{2,1,0:T(1,128)S(1)} %bitcast.201), channel_id=1, replica_groups=mesh['parts'=2,'rows'=16] {'rows'}, dimensions={0}, use_global_device_ids=true | all-gather | bytes 17408 | tf_op jit(solution)/shard_map/all_gather | solution.py:67
  160.2 11.1 collective-permute-start.58
  177.8 19.2 %fusion.6 = f32[32,128,256,1]{2,1,0,3:T(8,128)} fusion(f32[32,128,3,128]{3,1,0,2:T(8,128)S(1)} %bitcast.178, f32[32,3,256,128]{3,2,1,0:T(8,128)} %bitcast.177), kind=kOutput, calls=%fused_computation.19 | convolution fusion | flops 4831838208 | bytes 23068672 | tf_op jit(solution)/shard_map/rtkj,tckj->rtc/dot_general | solution.py:34
  202.4 13.0 %all-to-all-start = ((f32[256,16,256]{2,0,1:T(8,128)}), f32[256,16,256]{2,0,1:T(8,128)}, u32[]{:S(2)}, u32[]{:S(2)}) async-start(f32[256,16,256]{2,0,1:T(8,128)} %copy.135), calls=%async_computation | async-start | bytes 8388608 | tf_op jit(solution)/shard_map/all_to_all | solution.py:62
  216.9 93.4 %collective-permute-done.30 = f32[256,3,128]{2,0,1:T(8,128)S(1)} collective-permute-done((f32[256,3,128]{2,0,1:T(8,128)S(1)}, f32[256,3,128]{2,0,1:T(8,128)S(1)}, u32[]{:S(2)}, u32[]{:S(2)}) %collective-permute-start.30) | collective-permute-done | bytes 393248 | tf_op jit(solution)/shard_map/ppermute | solution.py:19
  396.9 15.1 %bitcast_add_fusion = (f32[256,32,128]{0,2,1:T(8,128)}, f32[32,128,256,1]{2,1,0,3:T(8,128)}) fusion(f32[256,32,128]{0,2,1:T(8,128)} %bitcast.187, f32[32,128,3,128]{3,1,0,2:T(8,128)} %bitcast.179, f32[32,3,128,256]{3,2,1,0:T(8,128)} %bitcast.180), kind=kOutput, calls=%fused_computation.30 | convolution fusion | flops 4832886784 | bytes 31457280 | tf_op jit(solution)/shard_map/tkjc,tqkj->ctq/dot_general | solution.py:43
  423.0 12.7 %copy.139 = f32[32,3,256,128]{3,2,0,1:T(8,128)} copy(f32[32,3,256,128]{2,3,1,0:T(8,128)} %bitcast.174) | data formatting | bytes 25165824 | tf_op jit(solution)/shard_map/gather | solution.py:32
  435.7 21.2 %fusion.4 = f32[32,128,256,1]{2,1,0,3:T(8,128)} fusion(f32[32,128,3,128]{3,1,0,2:T(8,128)} %bitcast.5, f32[32,3,256,128]{3,2,0,1:T(8,128)} %copy.139), kind=kOutput, calls=%fused_computation.17 | convolution fusion | flops 4831838208 | bytes 23068672 | tf_op jit(solution)/shard_map/rtkj,tckj->rtc/dot_general | solution.py:34
  473.7 93.4 %collective-permute-done.15 = f32[256,3,128]{2,0,1:T(8,128)S(1)} collective-permute-done((f32[256,3,128]{2,0,1:T(8,128)S(1)}, f32[256,3,128]{2,0,1:T(8,128)S(1)}, u32[]{:S(2)}, u32[]{:S(2)}) %collective-permute-start.15) | collective-permute-done | bytes 393248 | tf_op jit(solution)/shard_map/ppermute | solution.py:19
  643.0 15.0 %bitcast_add_fusion.1 = (f32[256,32,128]{0,2,1:T(8,128)}, f32[32,128,256,1]{2,1,0,3:T(8,128)}) fusion(f32[256,32,128]{0,2,1:T(8,128)} %bitcast.188, f32[32,128,3,128]{3,1,0,2:T(8,128)} %bitcast.5, f32[32,3,128,256]{3,2,1,0:T(8,128)} %bitcast.181), kind=kOutput, calls=%fused_computation.31 | convolution fusion | flops 4832886784 | bytes 31457280 | tf_op jit(solution)/shard_map/tkjc,tqkj->ctq/dot_general | solution.py:43
  669.1 12.9 %copy.144 = f32[32,3,256,128]{3,2,0,1:T(8,128)} copy(f32[32,3,256,128]{2,3,1,0:T(8,128)} %bitcast.175) | data formatting | bytes 25165824 | tf_op jit(solution)/shard_map/gather | solution.py:32
  682.0 21.2 %fusion.2 = f32[32,128,256,1]{2,1,0,3:T(8,128)} fusion(f32[32,128,3,128]{3,1,0,2:T(8,128)} %bitcast.3, f32[32,3,256,128]{3,2,0,1:T(8,128)} %copy.144), kind=kOutput, calls=%fused_computation.15 | convolution fusion | flops 4831838208 | bytes 23068672 | tf_op jit(solution)/shard_map/rtkj,tckj->rtc/dot_general | solution.py:34
  719.9 93.4 %collective-permute-done = f32[256,3,128]{2,0,1:T(8,128)S(1)} collective-permute-done((f32[256,3,128]{2,0,1:T(8,128)S(1)}, f32[256,3,128]{2,0,1:T(8,128)S(1)}, u32[]{:S(2)}, u32[]{:S(2)}) %collective-permute-start) | collective-permute-done | bytes 393248 | tf_op jit(solution)/shard_map/ppermute | solution.py:19
  890.2 15.0 %bitcast_add_fusion.2 = (f32[256,32,128]{0,2,1:T(8,128)}, f32[32,128,256,1]{2,1,0,3:T(8,128)}) fusion(f32[256,32,128]{0,2,1:T(8,128)} %bitcast.186, f32[32,128,3,128]{3,1,0,2:T(8,128)} %bitcast.3, f32[32,3,128,256]{3,2,1,0:T(8,128)} %bitcast.182), kind=kOutput, calls=%fused_computation.32 | convolution fusion | flops 4832886784 | bytes 31457280 | tf_op jit(solution)/shard_map/tkjc,tqkj->ctq/dot_general | solution.py:43
  905.2 11.1 gather_fusion.6
  916.3 12.7 %copy.149 = f32[32,3,256,128]{3,2,0,1:T(8,128)} copy(f32[32,3,256,128]{2,3,1,0:T(8,128)} %bitcast.176) | data formatting | bytes 25165824 | tf_op jit(solution)/shard_map/gather | solution.py:32
  929.1 21.2 %fusion = f32[32,128,256,1]{2,1,0,3:T(8,128)} fusion(f32[32,128,3,128]{3,1,0,2:T(8,128)} %bitcast.1, f32[32,3,256,128]{3,2,0,1:T(8,128)} %copy.149), kind=kOutput, calls=%fused_computation.13 | convolution fusion | flops 4831838208 | bytes 23068672 | tf_op jit(solution)/shard_map/rtkj,tckj->rtc/dot_general | solution.py:34
  983.4 74.8 %all-to-all-done.3 = f32[256,16,256]{2,0,1:T(8,128)} async-done(((f32[256,16,256]{2,0,1:T(8,128)}), f32[256,16,256]{2,0,1:T(8,128)}, u32[]{:S(2)}, u32[]{:S(2)}) %all-to-all-start.3) | async-done | bytes 4194336 | tf_op jit(solution)/shard_map/all_to_all | solution.py:62
  1058.2 11.1 gather_fusion.7
  1069.3 13.8 %fusion.8 = f32[32,128,256,1]{2,1,0,3:T(8,128)} fusion(f32[32,128,3,128]{3,1,0,2:T(8,128)} %bitcast.1, f32[32,3,128,256]{3,2,1,0:T(8,128)} %bitcast.183), kind=kOutput, calls=%fused_computation.21 | convolution fusion | flops 4831838208 | bytes 23068672 | tf_op jit(solution)/shard_map/tkjc,tqkj->ctq/dot_general | solution.py:43
  1088.7 16.3 %slice_add_fusion = (f32[1,256,4096]{2,1,0:T(8,128)S(1)}, f32[1,256,4096]{2,1,0:T(8,128)}, f32[1,256,4096]{2,1,0:T(8,128)}, f32[1,256,4096]{2,1,0:T(8,128)}) fusion(f32[1,256,4096]{2,1,0:T(8,128)} %copy.152, f32[4,256,4096]{2,1,0:T(8,128)} %param.11, f32[1,256,4096]{2,1,0:T(8,128)} %copy.155, f32[1,256,4096]{2,1,0:T(8,128)} %copy.154, f32[1,256,4096]{2,1,0:T(8,128)} %copy.153), kind=kLoop, calls=%fused_computation.33 | loop fusion | flops 4194304 | bytes 50331648 | tf_op jit(solution)/shard_map/add | solution.py:64
  (301 shorter events, 438.3 us)
Async XLA Ops:
  4.8 31.3 %collective-permute-start.46 = (f32[256,3,128]{2,0,1:T(8,128)S(1)}, f32[256,3,128]{2,0,1:T(8,128)}, u32[]{:S(2)}, u32[]{:S(2)}) collective-permute-start(f32[256,3,128]{2,0,1:T(8,128)S(1)} %get-tuple-element.23), channel_id=1, source_target_pairs={{0,15},{1,0},{2,1},{3,2},{4,3},{5,4},{6,5},{7,6},{8,7},{9,8},{10,9... | collective-permute-start | bytes 1179656 | tf_op jit(solution)/shard_map/ppermute | solution.py:22
  9.6 27.1 %collective-permute-start.47 = (f32[256,3,128]{2,0,1:T(8,128)}, f32[256,3,128]{2,0,1:T(8,128)}, u32[]{:S(2)}, u32[]{:S(2)}) collective-permute-start(f32[256,3,128]{2,0,1:T(8,128)} %collective-permute-done.45), channel_id=1, source_target_pairs={{0,1},{1,2},{2,3},{3,4},{4,5},{5,6},{6,7},{7,8},{8,9},{9,10},{10,1... | collective-permute-start | bytes 1179656 | tf_op jit(solution)/shard_map/ppermute | solution.py:19
  36.1 33.0 %collective-permute-start.48 = (f32[256,3,128]{2,0,1:T(8,128)}, f32[256,3,128]{2,0,1:T(8,128)S(1)}, u32[]{:S(2)}, u32[]{:S(2)}) collective-permute-start(f32[256,3,128]{2,0,1:T(8,128)} %collective-permute-done.46), channel_id=1, source_target_pairs={{0,15},{1,0},{2,1},{3,2},{4,3},{5,4},{6,5},{7,6},{8,7},{9,8},{10,9... | collective-permute-start | bytes 1179656 | tf_op jit(solution)/shard_map/ppermute | solution.py:22
  36.7 32.7 %collective-permute-start.49 = (f32[256,3,128]{2,0,1:T(8,128)}, f32[256,3,128]{2,0,1:T(8,128)}, u32[]{:S(2)}, u32[]{:S(2)}) collective-permute-start(f32[256,3,128]{2,0,1:T(8,128)} %collective-permute-done.47), channel_id=1, source_target_pairs={{0,1},{1,2},{2,3},{3,4},{4,5},{5,6},{6,7},{7,8},{8,9},{9,10},{10,1... | collective-permute-start | bytes 1179656 | tf_op jit(solution)/shard_map/ppermute | solution.py:19
  69.1 27.2 %collective-permute-start.50 = (f32[256,3,128]{2,0,1:T(8,128)S(1)}, f32[256,3,128]{2,0,1:T(8,128)}, u32[]{:S(2)}, u32[]{:S(2)}) collective-permute-start(f32[256,3,128]{2,0,1:T(8,128)S(1)} %collective-permute-done.48), channel_id=1, source_target_pairs={{0,15},{1,0},{2,1},{3,2},{4,3},{5,4},{6,5},{7,6},{8,7},{9,8},{10,9... | collective-permute-start | bytes 1179656 | tf_op jit(solution)/shard_map/ppermute | solution.py:22
  69.4 71.4 %collective-permute-start.51 = (f32[256,3,128]{2,0,1:T(8,128)}, f32[256,3,128]{2,0,1:T(8,128)}, u32[]{:S(2)}, u32[]{:S(2)}) collective-permute-start(f32[256,3,128]{2,0,1:T(8,128)} %collective-permute-done.49), channel_id=1, source_target_pairs={{0,1},{1,2},{2,3},{3,4},{4,5},{5,6},{6,7},{7,8},{8,9},{9,10},{10,1... | collective-permute-start | bytes 1179656 | tf_op jit(solution)/shard_map/ppermute | solution.py:19
  96.4 47.1 %collective-permute-start.52 = (f32[256,3,128]{2,0,1:T(8,128)}, f32[256,3,128]{2,0,1:T(8,128)}, u32[]{:S(2)}, u32[]{:S(2)}) collective-permute-start(f32[256,3,128]{2,0,1:T(8,128)} %collective-permute-done.50), channel_id=1, source_target_pairs={{0,15},{1,0},{2,1},{3,2},{4,3},{5,4},{6,5},{7,6},{8,7},{9,8},{10,9... | collective-permute-start | bytes 1179656 | tf_op jit(solution)/shard_map/ppermute | solution.py:22
  156.8 14.6 %collective-permute-start.57 = (f32[256,3,128]{2,0,1:T(8,128)S(1)}, f32[256,3,128]{2,0,1:T(8,128)S(1)}, u32[]{:S(2)}, u32[]{:S(2)}) collective-permute-start(f32[256,3,128]{2,0,1:T(8,128)S(1)} %collective-permute-done.55), channel_id=1, source_target_pairs={{0,1},{1,2},{2,3},{3,4},{4,5},{5,6},{6,7},{7,8},{8,9},{9,10},{10,1... | collective-permute-start | bytes 1179656 | tf_op jit(solution)/shard_map/ppermute | solution.py:19
  160.2 12.5 %collective-permute-start.58 = (f32[256,3,128]{2,0,1:T(8,128)S(1)}, f32[256,3,128]{2,0,1:T(8,128)S(1)}, u32[]{:S(2)}, u32[]{:S(2)}) collective-permute-start(f32[256,3,128]{2,0,1:T(8,128)S(1)} %collective-permute-done.56), channel_id=1, source_target_pairs={{0,15},{1,0},{2,1},{3,2},{4,3},{5,4},{6,5},{7,6},{8,7},{9,8},{10,9... | collective-permute-start | bytes 1179656 | tf_op jit(solution)/shard_map/ppermute | solution.py:22
  202.4 183.4 %all-to-all-start = ((f32[256,16,256]{2,0,1:T(8,128)}), f32[256,16,256]{2,0,1:T(8,128)}, u32[]{:S(2)}, u32[]{:S(2)}) async-start(f32[256,16,256]{2,0,1:T(8,128)} %copy.135), calls=%async_computation | async-start | bytes 8388608 | tf_op jit(solution)/shard_map/all_to_all | solution.py:62
  215.4 94.9 %collective-permute-start.30 = (f32[256,3,128]{2,0,1:T(8,128)S(1)}, f32[256,3,128]{2,0,1:T(8,128)S(1)}, u32[]{:S(2)}, u32[]{:S(2)}) collective-permute-start(f32[256,3,128]{2,0,1:T(8,128)S(1)} %copy-done.4), channel_id=1, source_target_pairs={{0,1},{1,2},{2,3},{3,4},{4,5},{5,6},{6,7},{7,8},{8,9},{9,10},{10,1... | collective-permute-start | bytes 1179656 | tf_op jit(solution)/shard_map/ppermute | solution.py:19
  216.9 96.8 %collective-permute-start.31 = (f32[256,3,128]{2,0,1:T(8,128)S(1)}, f32[256,3,128]{2,0,1:T(8,128)S(1)}, u32[]{:S(2)}, u32[]{:S(2)}) collective-permute-start(f32[256,3,128]{2,0,1:T(8,128)S(1)} %copy-done.4), channel_id=1, source_target_pairs={{0,15},{1,0},{2,1},{3,2},{4,3},{5,4},{6,5},{7,6},{8,7},{9,8},{10,9... | collective-permute-start | bytes 1179656 | tf_op jit(solution)/shard_map/ppermute | solution.py:22
  330.1 24.6 %collective-permute-start.37 = (f32[256,3,128]{2,0,1:T(8,128)S(1)}, f32[256,3,128]{2,0,1:T(8,128)S(1)}, u32[]{:S(2)}, u32[]{:S(2)}) collective-permute-start(f32[256,3,128]{2,0,1:T(8,128)S(1)} %collective-permute-done.35), channel_id=1, source_target_pairs={{0,15},{1,0},{2,1},{3,2},{4,3},{5,4},{6,5},{7,6},{8,7},{9,8},{10,9... | collective-permute-start | bytes 1179656 | tf_op jit(solution)/shard_map/ppermute | solution.py:22
  334.9 21.4 %collective-permute-start.38 = (f32[256,3,128]{2,0,1:T(8,128)S(1)}, f32[256,3,128]{2,0,1:T(8,128)}, u32[]{:S(2)}, u32[]{:S(2)}) collective-permute-start(f32[256,3,128]{2,0,1:T(8,128)S(1)} %collective-permute-done.36), channel_id=1, source_target_pairs={{0,1},{1,2},{2,3},{3,4},{4,5},{5,6},{6,7},{7,8},{8,9},{9,10},{10,1... | collective-permute-start | bytes 1179656 | tf_op jit(solution)/shard_map/ppermute | solution.py:19
  462.3 169.6 %all-to-all-start.1 = ((f32[256,16,256]{2,0,1:T(8,128)}), f32[256,16,256]{2,0,1:T(8,128)}, u32[]{:S(2)}, u32[]{:S(2)}) async-start(f32[256,16,256]{2,0,1:T(8,128)} %copy.140), calls=%async_computation.1 | async-start | bytes 8388608 | tf_op jit(solution)/shard_map/all_to_all | solution.py:62
  472.2 94.9 %collective-permute-start.15 = (f32[256,3,128]{2,0,1:T(8,128)S(1)}, f32[256,3,128]{2,0,1:T(8,128)S(1)}, u32[]{:S(2)}, u32[]{:S(2)}) collective-permute-start(f32[256,3,128]{2,0,1:T(8,128)S(1)} %copy-done.3), channel_id=1, source_target_pairs={{0,1},{1,2},{2,3},{3,4},{4,5},{5,6},{6,7},{7,8},{8,9},{9,10},{10,1... | collective-permute-start | bytes 1179656 | tf_op jit(solution)/shard_map/ppermute | solution.py:19
  473.7 96.8 %collective-permute-start.16 = (f32[256,3,128]{2,0,1:T(8,128)S(1)}, f32[256,3,128]{2,0,1:T(8,128)S(1)}, u32[]{:S(2)}, u32[]{:S(2)}) collective-permute-start(f32[256,3,128]{2,0,1:T(8,128)S(1)} %copy-done.3), channel_id=1, source_target_pairs={{0,15},{1,0},{2,1},{3,2},{4,3},{5,4},{6,5},{7,6},{8,7},{9,8},{10,9... | collective-permute-start | bytes 1179656 | tf_op jit(solution)/shard_map/ppermute | solution.py:22
  587.0 14.8 %collective-permute-start.22 = (f32[256,3,128]{2,0,1:T(8,128)S(1)}, f32[256,3,128]{2,0,1:T(8,128)S(1)}, u32[]{:S(2)}, u32[]{:S(2)}) collective-permute-start(f32[256,3,128]{2,0,1:T(8,128)S(1)} %collective-permute-done.20), channel_id=1, source_target_pairs={{0,15},{1,0},{2,1},{3,2},{4,3},{5,4},{6,5},{7,6},{8,7},{9,8},{10,9... | collective-permute-start | bytes 1179656 | tf_op jit(solution)/shard_map/ppermute | solution.py:22
  708.6 170.5 %all-to-all-start.2 = ((f32[256,16,256]{2,0,1:T(8,128)}), f32[256,16,256]{2,0,1:T(8,128)}, u32[]{:S(2)}, u32[]{:S(2)}) async-start(f32[256,16,256]{2,0,1:T(8,128)} %copy.145), calls=%async_computation.2 | async-start | bytes 8388608 | tf_op jit(solution)/shard_map/all_to_all | solution.py:62
  718.4 94.9 %collective-permute-start = (f32[256,3,128]{2,0,1:T(8,128)S(1)}, f32[256,3,128]{2,0,1:T(8,128)S(1)}, u32[]{:S(2)}, u32[]{:S(2)}) collective-permute-start(f32[256,3,128]{2,0,1:T(8,128)S(1)} %get-tuple-element.21), channel_id=1, source_target_pairs={{0,1},{1,2},{2,3},{3,4},{4,5},{5,6},{6,7},{7,8},{8,9},{9,10},{10,1... | collective-permute-start | bytes 1179656 | tf_op jit(solution)/shard_map/ppermute | solution.py:19
  719.9 96.8 %collective-permute-start.1 = (f32[256,3,128]{2,0,1:T(8,128)S(1)}, f32[256,3,128]{2,0,1:T(8,128)S(1)}, u32[]{:S(2)}, u32[]{:S(2)}) collective-permute-start(f32[256,3,128]{2,0,1:T(8,128)S(1)} %get-tuple-element.21), channel_id=1, source_target_pairs={{0,15},{1,0},{2,1},{3,2},{4,3},{5,4},{6,5},{7,6},{8,7},{9,8},{10,9... | collective-permute-start | bytes 1179656 | tf_op jit(solution)/shard_map/ppermute | solution.py:22
  833.2 16.1 %collective-permute-start.7 = (f32[256,3,128]{2,0,1:T(8,128)S(1)}, f32[256,3,128]{2,0,1:T(8,128)S(1)}, u32[]{:S(2)}, u32[]{:S(2)}) collective-permute-start(f32[256,3,128]{2,0,1:T(8,128)S(1)} %collective-permute-done.5), channel_id=1, source_target_pairs={{0,15},{1,0},{2,1},{3,2},{4,3},{5,4},{6,5},{7,6},{8,7},{9,8},{10,9... | collective-permute-start | bytes 1179656 | tf_op jit(solution)/shard_map/ppermute | solution.py:22
  837.9 12.1 %collective-permute-start.8 = (f32[256,3,128]{2,0,1:T(8,128)S(1)}, f32[256,3,128]{2,0,1:T(8,128)S(1)}, u32[]{:S(2)}, u32[]{:S(2)}) collective-permute-start(f32[256,3,128]{2,0,1:T(8,128)S(1)} %collective-permute-done.6), channel_id=1, source_target_pairs={{0,1},{1,2},{2,3},{3,4},{4,5},{5,6},{6,7},{7,8},{8,9},{9,10},{10,1... | collective-permute-start | bytes 1179656 | tf_op jit(solution)/shard_map/ppermute | solution.py:19
  955.6 102.6 %all-to-all-start.3 = ((f32[256,16,256]{2,0,1:T(8,128)}), f32[256,16,256]{2,0,1:T(8,128)}, u32[]{:S(2)}, u32[]{:S(2)}) async-start(f32[256,16,256]{2,0,1:T(8,128)} %copy.150), calls=%async_computation.3 | async-start | bytes 8388608 | tf_op jit(solution)/shard_map/all_to_all | solution.py:62
  (60 other events, 684.0 us)
